TPU v7x, 32 devices: a whole 2x2x4 slice. The times are simulated.
32 devices in a mesh: kv: 4 (over z), ep: 8 (over y, x, core).
Axes of the slice: x: 2, y: 2, z: 4, core: 2. Of those that a mesh axis runs over, the one named last changes fastest.
Arguments:
- queries: bfloat16 [8, 64, 2048], P('ep'), may hold values from -12 to 12
- new_keys: bfloat16 [8, 64, 512], P('ep'), may hold values from -12 to 12
- new_values: bfloat16 [8, 64, 512], P('ep'), may hold values from -6 to 6
- cache_keys: bfloat16 [8, 16, 128, 512], P('ep', 'kv'), may hold values from -12 to 12
- cache_values: bfloat16 [8, 16, 128, 512], P('ep', 'kv'), may hold values from -10 to 10
- page_table: int32 [8, 16], P('ep'), may hold values from 0 to 15, each once within a row
- cached_len: int32 [8], P('ep'), may hold values from 1 to 2048, 4096 in all
- moe_rows: bfloat16 [256, 4096], P('ep'), may hold values from -6 to 6
- expert_ids: int32 [256, 2], P('ep'), may hold values from 0 to 7, all different within a row; in each aligned block of 32 rows (0 to 31, 32 to 63, ...) at most 16 rows name the same one
- gate_probs: float32 [256, 2], P('ep'), may hold values from 0.1 to 0.9
- w_gate: bfloat16 [8, 4096, 8192], P('ep', None, 'kv'), may hold values from -0.09375 to 0.09375
- w_up: bfloat16 [8, 4096, 8192], P('ep', None, 'kv'), may hold values from -0.09375 to 0.09375
- w_down: bfloat16 [8, 8192, 4096], P('ep', 'kv'), may hold values from -0.09375 to 0.09375
Outputs:
- attn_out: bfloat16 [8, 64, 2048], P('ep')
- moe_out: bfloat16 [256, 4096], P('ep', 'kv')
Inputs may be any that keep to these rules, and one draw needn't show every extreme that they name: `page_table`: each row is a permutation of the 16 slots of its request. `cached_len`: cached positions at or past a request's length hold no data. `expert_ids`: each row names 2 different experts; among the 32 rows of one ep index no expert is named more than 16 times, and this bound is reached.
All inputs are finite; a program needn't handle non-finite values. No bound on the sum of `cached_len` on one device may be relied on, other than what follows from the above.
Results may differ from a plain program's by a relative error of at most 0.0085.
Values may be sent and summed in bfloat16 or wider, within the bound.
A program may use at most 128 MiB of HBM per device.

v0:
```python
import math

import jax
import jax.numpy as jnp
from jax import lax
from jax.sharding import PartitionSpec as P

HD = 128
EXPERTS = 8
TOP = 2
HQ = 16
KVH = 4
PAGE = 128
POOL_DEV = 4
CAP = 16


ROPE_BASE = 10000.0
MASKED = -1e30


def merged(part, axis, combine):
    gathered = jax.tree.map(lambda a: lax.all_gather(a, axis), part)

    def take(source):
        return jax.tree.map(lambda a: lax.dynamic_index_in_dim(a, source, 0, False), gathered)

    return lax.fori_loop(
        1, lax.axis_size(axis), lambda source, state: combine(state, take(source)), take(0)
    )


def rotary(values, positions):
    half_width = values.shape[-1] // 2
    indices = jnp.arange(half_width, dtype=jnp.float32)
    frequency = jnp.power(ROPE_BASE, -2.0 * indices / values.shape[-1])
    angles = positions.astype(jnp.float32)[:, None] * frequency[None, :]
    cosine = jnp.cos(angles)[:, None, :]
    sine_part = jnp.sin(angles)[:, None, :]
    lower_half = values[..., :half_width]
    upper_half = values[..., half_width:]
    return jnp.concatenate(
        [
            lower_half * cosine - upper_half * sine_part,
            upper_half * cosine + lower_half * sine_part,
        ],
        axis=-1,
    )


def combine_parts(first, second):
    high_first, total_first, blend_first = first
    high_second, total_second, blend_second = second
    highest = jnp.maximum(high_first, high_second)
    factor_first = jnp.exp(high_first - highest)
    factor_second = jnp.exp(high_second - highest)
    row_count, head_count = highest.shape
    blended = (
        blend_first.reshape(row_count, head_count, -1) * factor_first[..., None]
        + blend_second.reshape(row_count, head_count, -1) * factor_second[..., None]
    )
    return (
        highest,
        total_first * factor_first + total_second * factor_second,
        blended.reshape(blend_first.shape),
    )


def on_device(
    queries,
    new_keys,
    new_values,
    cache_keys,
    cache_values,
    page_table,
    cached_len,
    moe_rows,
    expert_ids,
    gate_probs,
    w_gate,
    w_up,
    w_down,
):
    kv_index = lax.axis_index("kv")
    kv_count = lax.axis_size("kv")
    all_rows = queries.shape[1]
    block_rows = all_rows // kv_count
    length = cached_len[0]
    group_size = HQ // KVH
    score_scale = 1.0 / math.sqrt(HD)
    slot_ids = kv_index * POOL_DEV + jnp.arange(POOL_DEV, dtype=jnp.int32)
    matches = (page_table[0][:, None] == slot_ids[None, :]).astype(jnp.int32)
    page_index = jnp.sum(
        matches * jnp.arange(page_table.shape[1], dtype=jnp.int32)[:, None], axis=0
    )
    cached_pos = (page_index[:, None] * PAGE + jnp.arange(PAGE, dtype=jnp.int32)[None, :]).reshape(
        -1
    )
    block_start = kv_index * block_rows
    own_pos = length + block_start + jnp.arange(block_rows, dtype=jnp.int32)
    key_block = lax.dynamic_slice_in_dim(new_keys[0], block_start, block_rows, 0)
    value_block = lax.dynamic_slice_in_dim(new_values[0], block_start, block_rows, 0)
    own_keys = rotary(key_block.astype(jnp.float32).reshape(block_rows, KVH, HD), own_pos).astype(
        jnp.bfloat16
    )
    local_keys = jnp.concatenate([cache_keys[0].reshape(-1, KVH, HD), own_keys], axis=0)
    local_values = jnp.concatenate(
        [cache_values[0].reshape(-1, KVH, HD), value_block.reshape(block_rows, KVH, HD)], axis=0
    )
    key_pos = jnp.concatenate([cached_pos, own_pos])
    live_keys = jnp.concatenate([cached_pos < length, jnp.ones((block_rows,), jnp.bool_)])
    positions = length + jnp.arange(all_rows, dtype=jnp.int32)
    rotated = rotary(queries[0].astype(jnp.float32).reshape(all_rows, HQ, HD), positions).astype(
        jnp.bfloat16
    )
    grouped = rotated.reshape(all_rows, KVH, group_size, HD)
    scores = (
        jnp.einsum("nkgd,mkd->nkgm", grouped, local_keys, preferred_element_type=jnp.float32)
        * score_scale
    )
    usable = (live_keys[None, :] & (key_pos[None, :] <= positions[:, None]))[:, None, None, :]
    scores = jnp.where(usable, scores, MASKED)
    part_high = jnp.max(scores, axis=-1)
    weights = jnp.where(usable, jnp.exp(scores - part_high[..., None]), 0.0)
    part_total = jnp.sum(weights, axis=-1)
    part_blend = jnp.einsum(
        "nkgm,mkd->nkgd",
        weights.astype(jnp.bfloat16),
        local_values,
        preferred_element_type=jnp.float32,
    )
    partials = (
        part_high.reshape(all_rows, HQ),
        part_total.reshape(all_rows, HQ),
        part_blend.reshape(all_rows, HQ * HD),
    )
    highest, row_total, blended = merged(partials, "kv", combine_parts)
    attn_out = (
        (blended.reshape(all_rows, HQ, HD) / row_total[..., None])
        .reshape(1, all_rows, HQ * HD)
        .astype(jnp.bfloat16)
    )
    ep_count = lax.axis_size("ep")
    share_count = ep_count // EXPERTS
    tok_rows = moe_rows.shape[0]
    slot_total = ep_count * CAP
    flat_ids = expert_ids.reshape(-1)
    one_hot = (flat_ids[:, None] == jnp.arange(EXPERTS, dtype=jnp.int32)[None, :]).astype(jnp.int32)
    earlier = jnp.cumsum(one_hot, axis=0) - one_hot
    slot_rank = jnp.sum(earlier * one_hot, axis=1)
    slot_index = jnp.arange(slot_total, dtype=jnp.int32)
    dest_expert = slot_index // CAP // share_count
    dest_slot = slot_index % CAP
    matched = (flat_ids[None, :] == dest_expert[:, None]) & (
        slot_rank[None, :] == dest_slot[:, None]
    )
    select = jnp.sum(matched.astype(jnp.float32).reshape(slot_total, tok_rows, TOP), axis=2).astype(
        jnp.bfloat16
    )
    weight_map = jnp.sum(
        jnp.where(matched, gate_probs.reshape(-1)[None, :], 0.0).reshape(slot_total, tok_rows, TOP),
        axis=2,
    )
    outgoing = (
        jnp.dot(select, moe_rows, preferred_element_type=jnp.float32)
        .astype(jnp.bfloat16)
        .reshape(ep_count, CAP, -1)
    )
    arrived = lax.all_to_all(outgoing, "ep", split_axis=0, concat_axis=0, tiled=True).reshape(
        slot_total, -1
    )
    gate_proj = jnp.dot(arrived, w_gate[0], preferred_element_type=jnp.float32)
    up_proj = jnp.dot(arrived, w_up[0], preferred_element_type=jnp.float32)
    hidden = (jax.nn.silu(gate_proj) * up_proj).astype(jnp.bfloat16)
    out_width = w_down.shape[2] // kv_count
    down_split = w_down[0].reshape(w_down.shape[1], kv_count, out_width)
    down_cols = lax.all_to_all(down_split, "kv", split_axis=1, concat_axis=0, tiled=True).reshape(
        -1, out_width
    )
    summed = jnp.dot(
        lax.all_gather(hidden, "kv", axis=1, tiled=True),
        down_cols,
        preferred_element_type=jnp.float32,
    )
    returned = (
        lax.all_to_all(
            summed.reshape(ep_count, CAP, -1).astype(jnp.bfloat16),
            "ep",
            split_axis=0,
            concat_axis=0,
            tiled=True,
        )
        .astype(jnp.float32)
        .reshape(slot_total, -1)
    )
    moe_out = jnp.dot(
        weight_map.T, returned, precision=lax.Precision.HIGHEST, preferred_element_type=jnp.float32
    ).astype(jnp.bfloat16)
    return (attn_out, moe_out)


def solution(mesh):
    return jax.shard_map(
        on_device,
        mesh=mesh,
        in_specs=(
            P("ep", None, None),
            P("ep", None, None),
            P("ep", None, None),
            P("ep", "kv", None, None),
            P("ep", "kv", None, None),
            P("ep", None),
            P("ep"),
            P("ep", None),
            P("ep", None),
            P("ep", None),
            P("ep", None, "kv"),
            P("ep", None, "kv"),
            P("ep", "kv", None),
        ),
        out_specs=(P("ep", None, None), P("ep", "kv")),
        check_vma=False,
    )
```

profile of v0, /device:TPU:0, one launch (start us, length us, event | category | flops | bytes accessed | tf_op | source)
XLA Modules:
  0.0 553.7 jit_solution(17547440977720222955)
XLA Ops:
  7.2 0.8 copy.65
  8.6 0.8 convert_reduce_fusion
  9.5 1.5 convolution_convert_fusion
  10.9 5.2 all-to-all-start
  16.1 27.9 %reshape_squeeze.11 = bf16[2048,4,1024]{2,1,0:T(4,128)(2,1)} reshape(bf16[1,2048,4096]{2,1,0:T(8,128)(2,1)} %param.27) | data formatting | bytes 33554432 | tf_op jit(solution)/shard_map/reshape;squeeze | solution.py:176
  44.0 17.0 %copy.67 = bf16[2048,4,1024]{2,0,1:T(8,128)(2,1)} copy(bf16[2048,4,1024]{2,1,0:T(4,128)(2,1)} %reshape_squeeze.11) | data formatting | bytes 33554432 | tf_op jit(solution)/shard_map/reshape;squeeze | solution.py:176
  61.0 7.1 %all-to-all-start.1 = ((bf16[2048,4,1024]{2,0,1:T(8,128)(2,1)}), bf16[2048,4,1024]{2,0,1:T(8,128)(2,1)}, u32[]{:S(2)}, u32[]{:S(2)}) async-start(bf16[2048,4,1024]{2,0,1:T(8,128)(2,1)} %copy.67), calls=%async_computation.1 | async-start | bytes 33554432 | tf_op jit(solution)/shard_map/all_to_all | solution.py:177
  68.9 0.7 dynamic-slice_convert_fusion
  71.3 0.2 fusion.44
  71.5 0.3 subtract_convert_fusion
  71.9 0.8 fusion.13
  72.6 0.8 fusion.19
  73.5 0.7 copy-done.2
  74.2 0.3 copy.63
  74.5 1.0 all_gather_reshape.11
  75.5 0.2 all-gather.5.cloned.1.call-start
  75.7 8.1 %fusion.5 = f32[128,2048]{1,0:T(8,128)S(1)} fusion(bf16[128,4096]{1,0:T(8,128)(2,1)S(1)} %bitcast.129, bf16[1,4096,2048]{2,1,0:T(8,128)(2,1)} %param.25), kind=kOutput, calls=%fused_computation.11 | convolution fusion | flops 2147483648 | bytes 18874368 | tf_op jit(solution)/shard_map/dot_general | solution.py:172
  83.8 9.5 %fusion.10 = bf16[128,2048]{1,0:T(8,128)(2,1)} fusion(bf16[128,4096]{1,0:T(8,128)(2,1)S(1)} %bitcast.130, bf16[1,4096,2048]{2,1,0:T(8,128)(2,1)} %param.26, f32[128,2048]{1,0:T(8,128)S(1)} %fusion.5), kind=kOutput, calls=%fused_computation.17 | convolution fusion | flops 2149056512 | bytes 19398656 | tf_op jit(solution)/shard_map/dot_general | solution.py:173
  93.4 2.6 fusion.15
  96.0 408.8 %all_gather.12 = f32[4,64,16]{1,2,0:T(8,128)S(1)} all-gather(f32[1,64,16]{1,2,0:T(8,128)S(1)} %bitcast.137), channel_id=1, replica_groups=mesh['kv'=4,'ep'=8] {'kv'}, dimensions={0}, use_global_device_ids=true | all-gather | bytes 20480 | tf_op jit(solution)/shard_map/all_gather | solution.py:23
  504.8 13.1 %all_gather.13 = f32[4,64,16]{1,2,0:T(8,128)S(1)} all-gather(f32[1,64,16]{1,2,0:T(8,128)S(1)} %bitcast.138), channel_id=1, replica_groups=mesh['kv'=4,'ep'=8] {'kv'}, dimensions={0}, use_global_device_ids=true | all-gather | bytes 20480 | tf_op jit(solution)/shard_map/all_gather | solution.py:23
  517.9 1.1 slice_bitcast_fusion
  519.0 6.6 %while.19 = (s32[]{:T(128)}, f32[64,16]{0,1:T(8,128)S(1)}, f32[64,16]{0,1:T(8,128)S(1)}, f32[64,2048]{1,0:T(8,128)S(1)}, f32[4,64,16]{1,2,0:T(8,128)S(1)}, /*ind...) while((s32[]{:T(128)}, f32[64,16]{0,1:T(8,128)S(1)}, ...), condition=%wide.region_4.5_spmd, body=%wide.region_3.4_spmd.sunk | while | flops 399365 | bytes 3727503 | solution.py:28
  519.4 0.2 mul.311
  519.6 1.6 fusion.57
  521.8 1.6 fusion.57
  524.0 1.6 fusion.57
  525.7 9.5 %convolution_convert_fusion.1 = bf16[8,16,1024]{2,1,0:T(8,128)(2,1)} fusion(bf16[8,16,8192]{2,1,0:T(8,128)(2,1)} %bitcast.132, bf16[8192,1024,1]{1,0,2:T(8,128)(2,1)} %bitcast.28), kind=kOutput, calls=%fused_computation.24 | convolution fusion | flops 2147614720 | bytes 19136512 | tf_op jit(solution)/shard_map/dot_general | solution.py:180
  535.2 3.8 all-to-all-start.2
  539.2 0.9 fusion.33
  540.1 5.8 %all-to-all-done.2 = bf16[8,16,1024]{2,1,0:T(8,128)(2,1)S(1)} async-done(((bf16[8,16,1024]{2,1,0:T(8,128)(2,1)}), bf16[8,16,1024]{2,1,0:T(8,128)(2,1)S(1)}, u32[]{:S(2)}, u32[]{:S(2)}) %all-to-all-start.2) | async-done | bytes 262176 | tf_op jit(solution)/shard_map/all_to_all | solution.py:186
  546.0 0.9 convolution_convert_fusion.2
  (69 shorter events, 4.1 us)
Async XLA Ops:
  7.2 2.3 copy-start
  10.9 50.1 %all-to-all-start = ((bf16[8,16,4096]{2,1,0:T(8,128)(2,1)}), bf16[8,16,4096]{2,1,0:T(8,128)(2,1)S(1)}, u32[]{:S(2)}, u32[]{:S(2)}) async-start(bf16[8,16,4096]{2,1,0:T(8,128)(2,1)} %bitcast.20), calls=%async_computation | async-start | bytes 2097152 | tf_op jit(solution)/shard_map/all_to_all | solution.py:169
  61.0 8.7 %copy-start.5 = (bf16[1,64,2048]{2,1,0:T(8,128)(2,1)S(1)}, bf16[1,64,2048]{2,1,0:T(8,128)(2,1)}, u32[]{:S(2)}) copy-start(bf16[1,64,2048]{2,1,0:T(8,128)(2,1)} %param.15) | copy-start | bytes 786436
  61.0 8.9 %copy-start.3 = (bf16[1,4,128,512]{3,2,1,0:T(8,128)(2,1)S(1)}, bf16[1,4,128,512]{3,2,1,0:T(8,128)(2,1)}, u32[]{:S(2)}) copy-start(bf16[1,4,128,512]{3,2,1,0:T(8,128)(2,1)} %param.18) | copy-start | bytes 1572868
  61.0 464.7 %all-to-all-start.1 = ((bf16[2048,4,1024]{2,0,1:T(8,128)(2,1)}), bf16[2048,4,1024]{2,0,1:T(8,128)(2,1)}, u32[]{:S(2)}, u32[]{:S(2)}) async-start(bf16[2048,4,1024]{2,0,1:T(8,128)(2,1)} %copy.67), calls=%async_computation.1 | async-start | bytes 33554432 | tf_op jit(solution)/shard_map/all_to_all | solution.py:177
  68.1 1.9 copy-start.4
  68.2 449.7 %all-gather.3.cloned.1.call-start = ((), (), s32[]{:S(2)}) async-start(), calls=%async_computation.3 | async-start | bytes 2621440 | tf_op jit(solution)/shard_map/all_gather | solution.py:23
  69.8 0.7 copy-start.6
  72.6 1.5 copy-start.2
  75.5 450.2 %all-gather.5.cloned.1.call-start = ((), (), s32[]{:S(2)}) async-start(), calls=%async_computation.4 | async-start | bytes 2621440 | tf_op jit(solution)/shard_map/all_gather | solution.py:181
  525.7 21.1 %copy-start.1 = (bf16[32,4096]{1,0:T(8,128)(2,1)S(1)}, bf16[32,4096]{1,0:T(8,128)(2,1)}, u32[]{:S(2)}) copy-start(bf16[32,4096]{1,0:T(8,128)(2,1)} %param.22) | copy-start | bytes 786436
  535.2 10.8 %all-to-all-start.2 = ((bf16[8,16,1024]{2,1,0:T(8,128)(2,1)}), bf16[8,16,1024]{2,1,0:T(8,128)(2,1)S(1)}, u32[]{:S(2)}, u32[]{:S(2)}) async-start(bf16[8,16,1024]{2,1,0:T(8,128)(2,1)} %convolution_convert_fusion.1), calls=%async_computation.2 | async-start | bytes 524288 | tf_op jit(solution)/shard_map/all_to_all | solution.py:186
Sparse Core Ops, SparseCore 0:
  75.6 138.6 all-gather.2
  215.9 74.2 all-gather.4
where the time goes:
time: 555 us; the launch traced here: 554 us
  blocking collectives  422 us (76%)
  local copies, waits for them, and re-layouts  51.9 us (9%)
  matrix products  31 us (6%)
  starting transfers between devices  16.4 us (3%)
  between operations  15 us (3%)
  other arithmetic  11.5 us (2%)
  waiting for transfers between devices  5.86 us (1%)
    all_gather x2, blocking collectives, merged(): gathered = jax.tree.map(lambda a: lax.all_gather(a, axis), part)  422 us
    another operation x2, local copies, waits for them, and re-layouts, on_device(): down_split = w_down[0].reshape(w_down.shape[1], kv_count, out_width)  44.9 us
  transfers between devices with their start and end apart: 5, of which 1 were waited for; matrix products, arithmetic and copies ran while one was open for 14% of the time, Pallas kernels for 0%

commit v1 on v0

v1 whole, which is shorter than its diff:
```python
import functools
import math

import jax
import jax.numpy as jnp
from jax import lax
from jax.experimental import pallas as pl
from jax.experimental.pallas import tpu as pltpu
from jax.sharding import PartitionSpec as P

HD = 128
EXPERTS = 8
HQ = 16
KVH = 4
PAGE = 128
CAP = 16
GROUP = HQ // KVH
K_CHUNKS = 4

ROPE_BASE = 10000.0
MASKED = -1e30
SCALE = 1.0 / math.sqrt(HD)
BF16 = jnp.bfloat16
F32 = jnp.float32
MESH = pl.DeviceIdType.MESH


def dot(a, b, dims=((1,), (0,))):
    return lax.dot_general(a, b, (dims, ((), ())), preferred_element_type=F32)


def kernel(
    n_kv,
    n_ep,
    length_ref,
    page_ref,
    queries_ref,
    new_keys_ref,
    new_values_ref,
    keys_ref,
    values_ref,
    trig_ref,
    rows_ref,
    route_ref,
    gate_hbm,
    up_hbm,
    down_hbm,
    attn_ref,
    moe_ref,
    gate_w,
    up_w,
    down_w,
    packed,
    arrived,
    gate_acc,
    up_acc,
    hidden,
    back_out,
    back_in,
    part_out,
    part_in,
    own_part,
    weights,
    blend_out,
    blend_in,
    stat_out,
    stat_in,
    final,
    gate_sem,
    up_sem,
    down_sem,
    row_send,
    row_recv,
    back_send,
    back_recv,
    part_send,
    part_recv,
    blend_send,
    blend_recv,
    stat_send,
    stat_recv,
    final_send,
    final_recv,
):
    kv = lax.axis_index("kv")
    ep = lax.axis_index("ep")
    new = queries_ref.shape[0]
    tok_rows, width = rows_ref.shape
    slots = n_ep * CAP
    depth = width // K_CHUNKS
    units = gate_acc.shape[1]
    out_width = moe_ref.shape[1]
    lanes = HQ * new // n_kv
    share = n_ep // EXPERTS

    def kv_peer(offset):
        return lax.rem(kv + offset, n_kv)

    def ep_peer(offset):
        return lax.rem(ep + offset, n_ep)

    def aligned(index, size):
        return pl.ds(pl.multiple_of(index * size, size), size)

    gate_copies = []
    up_copies = []
    for c in range(K_CHUNKS):
        part = pl.ds(c * depth, depth)
        gate_copies.append(
            pltpu.make_async_copy(gate_hbm.at[part], gate_w.at[part], gate_sem.at[c])
        )
        up_copies.append(pltpu.make_async_copy(up_hbm.at[part], up_w.at[part], up_sem.at[c]))
        gate_copies[c].start()
        up_copies[c].start()
    down_copies = []
    for i in range(n_kv):
        source = down_hbm.at[:, aligned(kv_peer(i + 1), out_width)]
        down_copies.append(pltpu.make_async_copy(source, down_w.at[i], down_sem.at[i]))
        down_copies[i].start()

    barrier = pltpu.get_barrier_semaphore()

    def greet(offset, carry):
        pl.semaphore_signal(
            barrier, inc=1, device_id={"ep": ep_peer(offset)}, device_id_type=MESH
        )
        return carry

    lax.fori_loop(1, n_ep, greet, 0)
    for offset in range(1, n_kv):
        pl.semaphore_signal(
            barrier, inc=1, device_id={"kv": kv_peer(offset)}, device_id_type=MESH
        )

    slot = lax.broadcasted_iota(jnp.int32, (slots, tok_rows), 0)
    expert = lax.div(slot, CAP * share).astype(F32)
    rank_wanted = lax.rem(slot, CAP).astype(F32)
    first = route_ref[0:1, :] == expert
    second = route_ref[1:2, :] == expert
    named = jnp.where(first | second, 1.0, 0.0)
    earlier = jnp.where(
        lax.broadcasted_iota(jnp.int32, (tok_rows, tok_rows), 0)
        < lax.broadcasted_iota(jnp.int32, (tok_rows, tok_rows), 1),
        1.0,
        0.0,
    )
    rank = dot(named.astype(BF16), earlier.astype(BF16))
    select = jnp.where(rank == rank_wanted, named, 0.0)
    prob = jnp.where(first, route_ref[2:3, :], 0.0) + jnp.where(second, route_ref[3:4, :], 0.0)
    weight = select * prob
    weight_high = weight.astype(BF16)
    weights[:, :tok_rows] = weight_high
    weights[:, tok_rows:] = (weight - weight_high.astype(F32)).astype(BF16)
    select = select.astype(BF16)
    for c in range(K_CHUNKS):
        packed[c] = dot(select, rows_ref[:, c * depth : (c + 1) * depth]).astype(BF16)
        arrived[c, aligned(ep, CAP)] = packed[c, aligned(ep, CAP)]

    pl.semaphore_wait(barrier, n_ep + n_kv - 2)

    def row_copy(c, offset):
        peer = ep_peer(offset)
        return pltpu.make_async_remote_copy(
            src_ref=packed.at[c, aligned(peer, CAP)],
            dst_ref=arrived.at[c, aligned(ep, CAP)],
            send_sem=row_send.at[c, offset],
            recv_sem=row_recv.at[c, offset],
            device_id={"ep": peer},
            device_id_type=MESH,
        )

    def row_landing(c, offset):
        source = ep_peer(n_ep - offset)
        return pltpu.make_async_remote_copy(
            src_ref=packed.at[c, aligned(source, CAP)],
            dst_ref=arrived.at[c, aligned(source, CAP)],
            send_sem=row_send.at[c, offset],
            recv_sem=row_recv.at[c, offset],
            device_id={"ep": source},
            device_id_type=MESH,
        )

    def each_peer(act):
        def step(offset, carry):
            act(offset)
            return carry

        lax.fori_loop(1, n_ep, step, 0)

    for c in range(K_CHUNKS):
        each_peer(lambda offset, c=c: row_copy(c, offset).start())

    length = length_ref[0]
    cosine = trig_ref[:, :HD]
    sine = trig_ref[:, HD:]

    def rotated(values):
        values = values.astype(F32)
        return (values * cosine + pltpu.roll(values, HD // 2, 1) * sine).astype(BF16)

    pool = keys_ref.shape[0] // PAGE
    group_lanes = GROUP * new
    live = []
    token = lax.broadcasted_iota(jnp.int32, (PAGE, group_lanes), 0)
    for s in range(pool):
        slot_id = kv * pool + s
        page = jnp.int32(0)
        for i in range(page_ref.shape[1]):
            page = page + jnp.where(page_ref[0, i] == slot_id, i, 0)
        live.append(token < length - page * PAGE)
    block = new // n_kv
    new_key = lax.broadcasted_iota(jnp.int32, (new, group_lanes), 0)
    new_query = lax.rem(lax.broadcasted_iota(jnp.int32, (new, group_lanes), 1), new)
    new_live = (new_key <= new_query) & (new_key >= kv * block) & (new_key < (kv + 1) * block)

    for g in range(KVH):
        column = slice(g * HD, (g + 1) * HD)
        grouped = jnp.concatenate(
            [
                rotated(queries_ref[:, h * HD : (h + 1) * HD])
                for h in range(g * GROUP, (g + 1) * GROUP)
            ],
            axis=0,
        )
        nt = ((1,), (1,))
        tn = ((0,), (0,))
        cached = [
            jnp.where(
                live[s],
                dot(keys_ref[s * PAGE : (s + 1) * PAGE, column], grouped, nt) * SCALE,
                MASKED,
            )
            for s in range(pool)
        ]
        fresh = jnp.where(
            new_live, dot(rotated(new_keys_ref[:, column]), grouped, nt) * SCALE, MASKED
        )
        high = jnp.max(fresh, axis=0, keepdims=True)
        for s in range(pool):
            high = jnp.maximum(high, jnp.max(cached[s], axis=0, keepdims=True))
        probs = jnp.where(new_live, jnp.exp(fresh - high), 0.0)
        total = jnp.sum(probs, axis=0, keepdims=True)
        blend = dot(new_values_ref[:, column], probs.astype(BF16), tn)
        for s in range(pool):
            probs = jnp.where(live[s], jnp.exp(cached[s] - high), 0.0)
            total = total + jnp.sum(probs, axis=0, keepdims=True)
            blend = blend + dot(
                values_ref[s * PAGE : (s + 1) * PAGE, column], probs.astype(BF16), tn
            )
        for piece in range(group_lanes // lanes):
            owner = (g * group_lanes) // lanes + piece
            cut = slice(piece * lanes, (piece + 1) * lanes)
            blend_out[owner] = blend[:, cut].astype(BF16)
            stat_out[owner, 0:1] = high[:, cut]
            stat_out[owner, 1:2] = total[:, cut]

    def blend_copies(offset):
        peer = kv_peer(offset)
        blends = pltpu.make_async_remote_copy(
            src_ref=blend_out.at[peer],
            dst_ref=blend_in.at[offset],
            send_sem=blend_send.at[offset],
            recv_sem=blend_recv.at[offset],
            device_id={"kv": peer},
            device_id_type=MESH,
        )
        stats = pltpu.make_async_remote_copy(
            src_ref=stat_out.at[peer],
            dst_ref=stat_in.at[offset],
            send_sem=stat_send.at[offset],
            recv_sem=stat_recv.at[offset],
            device_id={"kv": peer},
            device_id_type=MESH,
        )
        return blends, stats

    for offset in range(1, n_kv):
        for copy in blend_copies(offset):
            copy.start()

    chunk = min(512, units)

    def project(c):
        gate_copies[c].wait()
        up_copies[c].wait()
        each_peer(lambda offset: row_landing(c, offset).wait_recv())

        def step(n, carry):
            cols = aligned(n, chunk)
            rows = slice(c * depth, (c + 1) * depth)
            gate = dot(arrived[c], gate_w[rows, cols])
            up = dot(arrived[c], up_w[rows, cols])
            if c:
                gate = gate + gate_acc[:, cols]
                up = up + up_acc[:, cols]
            if c == K_CHUNKS - 1:
                hidden[:, cols] = (gate / (1.0 + jnp.exp(-gate)) * up).astype(BF16)
            else:
                gate_acc[:, cols] = gate
                up_acc[:, cols] = up
            return carry

        lax.fori_loop(0, units // chunk, step, 0)

    def final_copy(offset):
        peer = kv_peer(offset)
        return pltpu.make_async_remote_copy(
            src_ref=final.at[kv],
            dst_ref=final.at[kv],
            send_sem=final_send.at[offset],
            recv_sem=final_recv.at[offset],
            device_id={"kv": peer},
            device_id_type=MESH,
        )

    def final_landing(offset):
        source = kv_peer(n_kv - offset)
        return pltpu.make_async_remote_copy(
            src_ref=final.at[source],
            dst_ref=final.at[source],
            send_sem=final_send.at[offset],
            recv_sem=final_recv.at[offset],
            device_id={"kv": source},
            device_id_type=MESH,
        )

    def merge():
        for offset in range(1, n_kv):
            for copy in blend_copies(offset):
                copy.wait_recv()
        highs = [stat_out[kv, 0:1]] + [stat_in[o, 0:1] for o in range(1, n_kv)]
        totals = [stat_out[kv, 1:2]] + [stat_in[o, 1:2] for o in range(1, n_kv)]
        blends = [blend_out[kv]] + [blend_in[o] for o in range(1, n_kv)]
        highest = functools.reduce(jnp.maximum, highs)
        factors = [jnp.exp(high - highest) for high in highs]
        total = sum(f * t for f, t in zip(factors, totals))
        blended = sum(f * b.astype(F32) for f, b in zip(factors, blends))
        turned = (blended / total).T.astype(BF16)
        for h in range(lanes // new):
            final[kv, :, h * HD : (h + 1) * HD] = turned[h * new : (h + 1) * new]
        for offset in range(1, n_kv):
            final_copy(offset).start()

    project(0)
    merge()
    for c in range(1, K_CHUNKS):
        project(c)

    def back_copy(i, offset):
        peer = ep_peer(offset)
        return pltpu.make_async_remote_copy(
            src_ref=back_out.at[i, aligned(peer, CAP)],
            dst_ref=back_in.at[i, aligned(ep, CAP)],
            send_sem=back_send.at[i, offset],
            recv_sem=back_recv.at[i, offset],
            device_id={"ep": peer},
            device_id_type=MESH,
        )

    def back_landing(i, offset):
        source = ep_peer(n_ep - offset)
        return pltpu.make_async_remote_copy(
            src_ref=back_out.at[i, aligned(source, CAP)],
            dst_ref=back_in.at[i, aligned(source, CAP)],
            send_sem=back_send.at[i, offset],
            recv_sem=back_recv.at[i, offset],
            device_id={"ep": source},
            device_id_type=MESH,
        )

    out_chunk = min(512, out_width)
    for i in range(n_kv):
        down_copies[i].wait()

        def step(n, carry, i=i):
            cols = aligned(n, out_chunk)
            back_out[i, :, cols] = dot(hidden[...], down_w[i, :, cols]).astype(BF16)
            return carry

        lax.fori_loop(0, out_width // out_chunk, step, 0)
        back_in[i, aligned(ep, CAP)] = back_out[i, aligned(ep, CAP)]
        each_peer(lambda offset, i=i: back_copy(i, offset).start())

    def part_copy(i):
        return pltpu.make_async_remote_copy(
            src_ref=part_out.at[i],
            dst_ref=part_in.at[i],
            send_sem=part_send.at[i],
            recv_sem=part_recv.at[i],
            device_id={"kv": kv_peer(i + 1)},
            device_id_type=MESH,
        )

    for i in range(n_kv):
        each_peer(lambda offset, i=i: back_landing(i, offset).wait_recv())
        mixed = dot(weights[...], back_in[i], ((0,), (0,)))
        mixed = mixed[:tok_rows] + mixed[tok_rows:]
        if i < n_kv - 1:
            part_out[i] = mixed.astype(BF16)
            part_copy(i).start()
        else:
            own_part[...] = mixed

    for offset in range(1, n_kv):
        final_landing(offset).wait_recv()
    for k in range(n_kv):
        attn_ref[:, k * lanes * HD // new : (k + 1) * lanes * HD // new] = final[k]

    result = own_part[...]
    for i in range(n_kv - 1):
        part_copy(i).wait_recv()
        result = result + part_in[i].astype(F32)
    moe_ref[...] = result.astype(BF16)

    for c in range(K_CHUNKS):
        each_peer(lambda offset, c=c: row_copy(c, offset).wait_send())
    for i in range(n_kv):
        each_peer(lambda offset, i=i: back_copy(i, offset).wait_send())
    for i in range(n_kv - 1):
        part_copy(i).wait_send()
    for offset in range(1, n_kv):
        for copy in blend_copies(offset):
            copy.wait_send()
        final_copy(offset).wait_send()


def on_device(
    queries,
    new_keys,
    new_values,
    cache_keys,
    cache_values,
    page_table,
    cached_len,
    moe_rows,
    expert_ids,
    gate_probs,
    w_gate,
    w_up,
    w_down,
):
    n_kv = lax.axis_size("kv")
    n_ep = lax.axis_size("ep")
    new = queries.shape[1]
    tok_rows, width = moe_rows.shape
    units = w_gate.shape[2]
    out_width = width // n_kv
    slots = n_ep * CAP
    depth = width // K_CHUNKS
    lanes = HQ * new // n_kv

    half = HD // 2
    frequency = jnp.power(ROPE_BASE, -2.0 * jnp.arange(half, dtype=F32) / HD)
    positions = cached_len[0] + jnp.arange(new, dtype=jnp.int32)
    angles = positions.astype(F32)[:, None] * frequency[None, :]
    cosine = jnp.cos(angles)
    sine = jnp.sin(angles)
    trig = jnp.concatenate([cosine, cosine, -sine, sine], axis=1)
    route = jnp.concatenate([expert_ids.T.astype(F32), gate_probs.T], axis=0)

    vmem = pl.BlockSpec(memory_space=pltpu.VMEM)
    smem = pl.BlockSpec(memory_space=pltpu.SMEM)
    hbm = pl.BlockSpec(memory_space=pl.ANY)
    dma = pltpu.SemaphoreType.DMA
    attn_out, moe_out = pl.pallas_call(
        functools.partial(kernel, n_kv, n_ep),
        out_shape=(
            jax.ShapeDtypeStruct((new, HQ * HD), BF16),
            jax.ShapeDtypeStruct((tok_rows, out_width), BF16),
        ),
        in_specs=[smem, smem] + [vmem] * 8 + [hbm] * 3,
        out_specs=(vmem, vmem),
        scratch_shapes=[
            pltpu.VMEM((width, units), BF16),
            pltpu.VMEM((width, units), BF16),
            pltpu.VMEM((n_kv, units, out_width), BF16),
            pltpu.VMEM((K_CHUNKS, slots, depth), BF16),
            pltpu.VMEM((K_CHUNKS, slots, depth), BF16),
            pltpu.VMEM((slots, units), F32),
            pltpu.VMEM((slots, units), F32),
            pltpu.VMEM((slots, units), BF16),
            pltpu.VMEM((n_kv, slots, out_width), BF16),
            pltpu.VMEM((n_kv, slots, out_width), BF16),
            pltpu.VMEM((n_kv - 1, tok_rows, out_width), BF16),
            pltpu.VMEM((n_kv - 1, tok_rows, out_width), BF16),
            pltpu.VMEM((tok_rows, out_width), F32),
            pltpu.VMEM((slots, 2 * tok_rows), BF16),
            pltpu.VMEM((n_kv, HD, lanes), BF16),
            pltpu.VMEM((n_kv, HD, lanes), BF16),
            pltpu.VMEM((n_kv, 8, lanes), F32),
            pltpu.VMEM((n_kv, 8, lanes), F32),
            pltpu.VMEM((n_kv, new, HQ * HD // n_kv), BF16),
            dma((K_CHUNKS,)),
            dma((K_CHUNKS,)),
            dma((n_kv,)),
            dma((K_CHUNKS, n_ep)),
            dma((K_CHUNKS, n_ep)),
            dma((n_kv, n_ep)),
            dma((n_kv, n_ep)),
            dma((n_kv,)),
            dma((n_kv,)),
            dma((n_kv,)),
            dma((n_kv,)),
            dma((n_kv,)),
            dma((n_kv,)),
            dma((n_kv,)),
            dma((n_kv,)),
        ],
        compiler_params=pltpu.CompilerParams(
            collective_id=0, has_side_effects=True, vmem_limit_bytes=60 * 1024 * 1024
        ),
    )(
        cached_len,
        page_table,
        queries[0],
        new_keys[0],
        new_values[0],
        cache_keys.reshape(-1, KVH * HD),
        cache_values.reshape(-1, KVH * HD),
        trig,
        moe_rows,
        route,
        w_gate[0],
        w_up[0],
        w_down[0],
    )
    return attn_out[None], moe_out


def solution(mesh):
    return jax.shard_map(
        on_device,
        mesh=mesh,
        in_specs=(
            P("ep", None, None),
            P("ep", None, None),
            P("ep", None, None),
            P("ep", "kv", None, None),
            P("ep", "kv", None, None),
            P("ep", None),
            P("ep"),
            P("ep", None),
            P("ep", None),
            P("ep", None),
            P("ep", None, "kv"),
            P("ep", None, "kv"),
            P("ep", "kv", None),
        ),
        out_specs=(P("ep", None, None), P("ep", "kv")),
        check_vma=False,
    )
```

time: 555 us -> 47.7 us (0.09)
  blocking collectives: 422 us -> 0 us
  local copies, waits for them, and re-layouts: 51.9 us -> 3.14 us
  Pallas kernels: 0 us -> 40.1 us
  matrix products: 31 us -> 0 us
  starting transfers between devices: 16.4 us -> 0 us
  between operations: 15 us -> 1.3 us
  other arithmetic: 11.5 us -> 2.88 us
  waiting for transfers between devices: 5.86 us -> 0 us
    all_gather x2 -> x0, blocking collectives: 422 us -> none  [merged(): gathered = jax.tree.map(lambda a: lax.all_gather(a, axis), part)]
    another operation x7 -> x0, local copies, waits for them, and re-layouts: 46.3 us -> none  [the longest x2 44.9 us: on_device(): down_split = w_down[0].reshape(w_down.shape[1], kv_count, out_width)]
    pallas_call x0 -> x1, Pallas kernels: none -> 40.1 us  [on_device(): pl.pallas_call(functools.partial(kernel, n_kv, n_ep), out_shape=(jax.Shap...]
    dot_general x7 -> x0, matrix products: 31 us -> none  [the longest x1 9.5 us: on_device(): up_proj = jnp.dot(arrived, w_up[0], preferred_element_type=jnp.float32)]
    all_to_all x3 -> x0, starting transfers between devices: 16.1 us -> none  [the longest x1 7.12 us: on_device(): lax.all_to_all(down_split, 'kv', split_axis=1, concat_axis=0, tiled=True)]
    all_to_all x3 -> x0, waiting for transfers between devices: 5.82 us -> none  [the longest x1 5.81 us: on_device(): lax.all_to_all(summed.reshape(ep_count, CAP, -1).astype(jnp.bfloat16), 'e...]
  transfers between devices with their start and end apart: 5 -> 0, of which waited for: 1 -> 0; matrix products, arithmetic and copies ran while one was open for 14% -> 0% of each run, Pallas kernels for 0% -> 0%
where the time goes in v1:
time: 47.7 us; the launch traced here: 47.4 us
  Pallas kernels  40.1 us (84%)
  local copies, waits for them, and re-layouts  3.14 us (7%)
  other arithmetic  2.88 us (6%)
  between operations  1.3 us (3%)
    pallas_call x1, Pallas kernels, on_device(): pl.pallas_call(functools.partial(kernel, n_kv, n_ep), out_shape=(jax.Shap...  40.1 us
    unnamed x2, local copies, waits for them, and re-layouts  3.14 us
    concatenate x1, other arithmetic, on_device(): route = jnp.concatenate([expert_ids.T.astype(F32), gate_probs.T], axis=0)  1.26 us

profile of v1, /device:TPU:0, one launch (start us, length us, event | category | flops | bytes accessed | tf_op | source)
XLA Modules:
  0.0 47.4 jit_solution(13948858485037736316)
XLA Ops:
  1.3 0.7 %convert_bitcast_fusion = f32[2,32]{1,0:T(2,128)S(1)} fusion(s32[32,2]{0,1:T(2,128)} %param.21), kind=kLoop, calls=%fused_computation.5 | loop fusion | flops 64 | bytes 512 | tf_op jit(solution)/shard_map/convert_element_type | solution.py:459
  2.0 1.3 %pad_maximum_fusion.1.route_ref = f32[4,32]{1,0:T(4,128)} fusion(f32[2,32]{1,0:T(2,128)} %bitcast.23, f32[2,32]{1,0:T(2,128)S(1)} %convert_bitcast_fusion), kind=kLoop, calls=%fused_computation.4 | loop fusion | flops 128 | bytes 1024 | tf_op jit(solution)/shard_map/concatenate | solution.py:459
  3.2 0.2 multiply_cosine_fusion
  3.4 0.7 %pad_maximum_fusion.trig_ref = f32[64,256]{1,0:T(8,128)} fusion(f32[64,64]{1,0:T(8,128)S(1)} %get-tuple-element.8, f32[64,64]{1,0:T(8,128)S(1)} %get-tuple-element.7, f32[64,64]{1,0:T(8,128)S(1)} %get-tuple-element.6), kind=kLoop, calls=%fused_computation | loop fusion | flops 49152 | bytes 114688 | tf_op jit(solution)/shard_map/concatenate | solution.py:458
  4.2 40.1 %shard_map.140 = (bf16[64,2048]{1,0:T(8,128)(2,1)}, bf16[32,1024]{1,0:T(8,128)(2,1)}) custom-call(s32[1]{0:T(128)} %copy.17.length_ref, s32[1,16]{1,0:T(1,128)} %page_ref.1, bf16[64,2048]{1,0:T(8,128)(2,1)} %bitcast.19, bf16[64,512]{1,0:T(8,128)(2,1)} %bitcast.21, bf16[64,512]{1,0:T(8,128)(2,1)} %bitcast.22, bf16[512,512]{1,0:T(8,128)(2,1)} %bitcast.17, ...), custom_call_target="tpu_custom_call" | custom-call | tf_op jit(solution)/shard_map/pallas_call | solution.py:465
  44.3 1.7 %copy.18 = bf16[1,64,2048]{2,1,0:T(8,128)(2,1)} copy(bf16[1,64,2048]{2,1,0:T(8,128)(2,1)} %bitcast.20) | data formatting | bytes 524288
  45.9 1.5 %copy.19 = bf16[32,1024]{1,0:T(8,128)(2,1)} copy(bf16[32,1024]{1,0:T(8,128)(2,1)} %get-tuple-element.12) | data formatting | bytes 131072
  (2 shorter events, 0.0 us)

commit v2 on v1

--- a/solution.py
+++ b/solution.py
@@ -39,9 +39,11 @@
     new_values_ref,
     keys_ref,
     values_ref,
-    trig_ref,
+    cos_ref,
+    sin_ref,
     rows_ref,
-    route_ref,
+    ids_ref,
+    probs_ref,
     gate_hbm,
     up_hbm,
     down_hbm,
@@ -133,10 +135,10 @@
         )
 
     slot = lax.broadcasted_iota(jnp.int32, (slots, tok_rows), 0)
-    expert = lax.div(slot, CAP * share).astype(F32)
+    expert = lax.div(slot, CAP * share)
     rank_wanted = lax.rem(slot, CAP).astype(F32)
-    first = route_ref[0:1, :] == expert
-    second = route_ref[1:2, :] == expert
+    first = ids_ref[0:1, :] == expert
+    second = ids_ref[1:2, :] == expert
     named = jnp.where(first | second, 1.0, 0.0)
     earlier = jnp.where(
         lax.broadcasted_iota(jnp.int32, (tok_rows, tok_rows), 0)
@@ -146,7 +148,7 @@
     )
     rank = dot(named.astype(BF16), earlier.astype(BF16))
     select = jnp.where(rank == rank_wanted, named, 0.0)
-    prob = jnp.where(first, route_ref[2:3, :], 0.0) + jnp.where(second, route_ref[3:4, :], 0.0)
+    prob = jnp.where(first, probs_ref[0:1, :], 0.0) + jnp.where(second, probs_ref[1:2, :], 0.0)
     weight = select * prob
     weight_high = weight.astype(BF16)
     weights[:, :tok_rows] = weight_high
@@ -191,8 +193,8 @@
         each_peer(lambda offset, c=c: row_copy(c, offset).start())
 
     length = length_ref[0]
-    cosine = trig_ref[:, :HD]
-    sine = trig_ref[:, HD:]
+    cosine = jnp.concatenate([cos_ref[...], cos_ref[...]], axis=1)
+    sine = jnp.concatenate([-sin_ref[...], sin_ref[...]], axis=1)
 
     def rotated(values):
         values = values.astype(F32)
@@ -455,8 +457,6 @@
     angles = positions.astype(F32)[:, None] * frequency[None, :]
     cosine = jnp.cos(angles)
     sine = jnp.sin(angles)
-    trig = jnp.concatenate([cosine, cosine, -sine, sine], axis=1)
-    route = jnp.concatenate([expert_ids.T.astype(F32), gate_probs.T], axis=0)
 
     vmem = pl.BlockSpec(memory_space=pltpu.VMEM)
     smem = pl.BlockSpec(memory_space=pltpu.SMEM)
@@ -468,7 +468,7 @@
             jax.ShapeDtypeStruct((new, HQ * HD), BF16),
             jax.ShapeDtypeStruct((tok_rows, out_width), BF16),
         ),
-        in_specs=[smem, smem] + [vmem] * 8 + [hbm] * 3,
+        in_specs=[smem, smem] + [vmem] * 10 + [hbm] * 3,
         out_specs=(vmem, vmem),
         scratch_shapes=[
             pltpu.VMEM((width, units), BF16),
@@ -517,9 +517,11 @@
         new_values[0],
         cache_keys.reshape(-1, KVH * HD),
         cache_values.reshape(-1, KVH * HD),
-        trig,
+        cosine,
+        sine,
         moe_rows,
-        route,
+        expert_ids.T,
+        gate_probs.T,
         w_gate[0],
         w_up[0],
         w_down[0],

time: 47.7 us -> 45.4 us (0.952)
  other arithmetic: 2.88 us -> 0.84 us
    concatenate x2 -> x0, other arithmetic: 1.99 us -> none  [the longest x1 1.26 us: on_device(): route = jnp.concatenate([expert_ids.T.astype(F32), gate_probs.T], axis=0)]
    sin x0 -> x1, other arithmetic: none -> 0.83 us  [on_device(): sine = jnp.sin(angles)]
    convert_element_type x1 -> x0, other arithmetic: 0.68 us -> none  [on_device(): route = jnp.concatenate([expert_ids.T.astype(F32), gate_probs.T], axis=0)]
where the time goes in v2:
time: 45.4 us; the launch traced here: 45.1 us
  Pallas kernels  39.9 us (88%)
  local copies, waits for them, and re-layouts  3.14 us (7%)
  between operations  1.3 us (3%)
  other arithmetic  0.84 us (2%)
    pallas_call x1, Pallas kernels, on_device(): pl.pallas_call(functools.partial(kernel, n_kv, n_ep), out_shape=(jax.Shap...  39.9 us
    unnamed x2, local copies, waits for them, and re-layouts  3.14 us

profile of v2, /device:TPU:0, one launch (start us, length us, event | category | flops | bytes accessed | tf_op | source)
XLA Modules:
  0.0 45.1 jit_solution(16233169811030228365)
XLA Ops:
  1.3 0.8 %multiply_sine_fusion = (f32[64,64]{1,0:T(8,128)}, f32[64,64]{1,0:T(8,128)}) fusion(f32[64]{0:T(128)S(1)} %multiply_power_fusion, f32[64]{0:T(128)S(1)} %add_convert_fusion), kind=kLoop, calls=%fused_computation | loop fusion | flops 4096 | bytes 33280 | tf_op jit(solution)/shard_map/sin | solution.py:459
  2.1 39.9 %shard_map.140 = (bf16[64,2048]{1,0:T(8,128)(2,1)}, bf16[32,1024]{1,0:T(8,128)(2,1)}) custom-call(s32[1]{0:T(128)} %copy.17.length_ref, s32[1,16]{1,0:T(1,128)} %page_ref.1, bf16[64,2048]{1,0:T(8,128)(2,1)} %bitcast.18, bf16[64,512]{1,0:T(8,128)(2,1)} %bitcast.20, bf16[64,512]{1,0:T(8,128)(2,1)} %bitcast.21, bf16[512,512]{1,0:T(8,128)(2,1)} %bitcast.16, ...), custom_call_target="tpu_custom_call" | custom-call | tf_op jit(solution)/shard_map/pallas_call | solution.py:465
  42.0 1.7 %copy.18 = bf16[1,64,2048]{2,1,0:T(8,128)(2,1)} copy(bf16[1,64,2048]{2,1,0:T(8,128)(2,1)} %bitcast.19) | data formatting | bytes 524288
  43.7 1.5 %copy.19 = bf16[32,1024]{1,0:T(8,128)(2,1)} copy(bf16[32,1024]{1,0:T(8,128)(2,1)} %get-tuple-element.11) | data formatting | bytes 131072
  (2 shorter events, 0.0 us)

commit v3 on v2

--- a/solution.py
+++ b/solution.py
@@ -34,11 +34,11 @@
     n_ep,
     length_ref,
     page_ref,
-    queries_ref,
-    new_keys_ref,
-    new_values_ref,
-    keys_ref,
-    values_ref,
+    queries_hbm,
+    new_keys_hbm,
+    new_values_hbm,
+    keys_hbm,
+    values_hbm,
     cos_ref,
     sin_ref,
     rows_ref,
@@ -47,8 +47,13 @@
     gate_hbm,
     up_hbm,
     down_hbm,
-    attn_ref,
+    attn_hbm,
     moe_ref,
+    queries_ref,
+    new_keys_ref,
+    new_values_ref,
+    keys_ref,
+    values_ref,
     gate_w,
     up_w,
     down_w,
@@ -68,6 +73,8 @@
     stat_out,
     stat_in,
     final,
+    load_sem,
+    store_sem,
     gate_sem,
     up_sem,
     down_sem,
@@ -104,6 +111,21 @@
     def aligned(index, size):
         return pl.ds(pl.multiple_of(index * size, size), size)
 
+    loads = [
+        pltpu.make_async_copy(source, target, load_sem.at[i])
+        for i, (source, target) in enumerate(
+            [
+                (queries_hbm, queries_ref),
+                (new_keys_hbm, new_keys_ref),
+                (new_values_hbm, new_values_ref),
+                (keys_hbm, keys_ref),
+                (values_hbm, values_ref),
+            ]
+        )
+    ]
+    for load in loads:
+        load.start()
+
     gate_copies = []
     up_copies = []
     for c in range(K_CHUNKS):
@@ -192,6 +214,8 @@
     for c in range(K_CHUNKS):
         each_peer(lambda offset, c=c: row_copy(c, offset).start())
 
+    for load in loads:
+        load.wait()
     length = length_ref[0]
     cosine = jnp.concatenate([cos_ref[...], cos_ref[...]], axis=1)
     sine = jnp.concatenate([-sin_ref[...], sin_ref[...]], axis=1)
@@ -383,6 +407,18 @@
         back_in[i, aligned(ep, CAP)] = back_out[i, aligned(ep, CAP)]
         each_peer(lambda offset, i=i: back_copy(i, offset).start())
 
+    for offset in range(1, n_kv):
+        final_landing(offset).wait_recv()
+    span = lanes * HD // new
+    stores = [
+        pltpu.make_async_copy(
+            final.at[k], attn_hbm.at[:, pl.ds(k * span, span)], store_sem.at[k]
+        )
+        for k in range(n_kv)
+    ]
+    for store in stores:
+        store.start()
+
     def part_copy(i):
         return pltpu.make_async_remote_copy(
             src_ref=part_out.at[i],
@@ -403,17 +439,14 @@
         else:
             own_part[...] = mixed
 
-    for offset in range(1, n_kv):
-        final_landing(offset).wait_recv()
-    for k in range(n_kv):
-        attn_ref[:, k * lanes * HD // new : (k + 1) * lanes * HD // new] = final[k]
-
     result = own_part[...]
     for i in range(n_kv - 1):
         part_copy(i).wait_recv()
         result = result + part_in[i].astype(F32)
     moe_ref[...] = result.astype(BF16)
 
+    for store in stores:
+        store.wait()
     for c in range(K_CHUNKS):
         each_peer(lambda offset, c=c: row_copy(c, offset).wait_send())
     for i in range(n_kv):
@@ -458,6 +491,7 @@
     cosine = jnp.cos(angles)
     sine = jnp.sin(angles)
 
+    keys = cache_keys.reshape(-1, KVH * HD)
     vmem = pl.BlockSpec(memory_space=pltpu.VMEM)
     smem = pl.BlockSpec(memory_space=pltpu.SMEM)
     hbm = pl.BlockSpec(memory_space=pl.ANY)
@@ -468,9 +502,14 @@
             jax.ShapeDtypeStruct((new, HQ * HD), BF16),
             jax.ShapeDtypeStruct((tok_rows, out_width), BF16),
         ),
-        in_specs=[smem, smem] + [vmem] * 10 + [hbm] * 3,
-        out_specs=(vmem, vmem),
+        in_specs=[smem, smem] + [hbm] * 5 + [vmem] * 5 + [hbm] * 3,
+        out_specs=(hbm, vmem),
         scratch_shapes=[
+            pltpu.VMEM((new, HQ * HD), BF16),
+            pltpu.VMEM((new, KVH * HD), BF16),
+            pltpu.VMEM((new, KVH * HD), BF16),
+            pltpu.VMEM(keys.shape, BF16),
+            pltpu.VMEM(keys.shape, BF16),
             pltpu.VMEM((width, units), BF16),
             pltpu.VMEM((width, units), BF16),
             pltpu.VMEM((n_kv, units, out_width), BF16),
@@ -490,6 +529,8 @@
             pltpu.VMEM((n_kv, 8, lanes), F32),
             pltpu.VMEM((n_kv, 8, lanes), F32),
             pltpu.VMEM((n_kv, new, HQ * HD // n_kv), BF16),
+            dma((5,)),
+            dma((n_kv,)),
             dma((K_CHUNKS,)),
             dma((K_CHUNKS,)),
             dma((n_kv,)),
@@ -515,7 +556,7 @@
         queries[0],
         new_keys[0],
         new_values[0],
-        cache_keys.reshape(-1, KVH * HD),
+        keys,
         cache_values.reshape(-1, KVH * HD),
         cosine,
         sine,

time: 45.4 us -> 55 us (1.21)
  Pallas kernels: 39.9 us -> 49.5 us
    pallas_call x1, Pallas kernels: 39.9 us -> 49.5 us  [on_device(): pl.pallas_call(functools.partial(kernel, n_kv, n_ep), out_shape=(jax.Shap...]
where the time goes in v3:
time: 55 us; the launch traced here: 54.8 us
  Pallas kernels  49.5 us (90%)
  local copies, waits for them, and re-layouts  3.14 us (6%)
  between operations  1.3 us (2%)
  other arithmetic  0.84 us (2%)
    pallas_call x1, Pallas kernels, on_device(): pl.pallas_call(functools.partial(kernel, n_kv, n_ep), out_shape=(jax.Shap...  49.5 us
    unnamed x2, local copies, waits for them, and re-layouts  3.14 us

profile of v3, /device:TPU:0, one launch (start us, length us, event | category | flops | bytes accessed | tf_op | source)
XLA Modules:
  0.0 54.8 jit_solution(17756661653086325968)
XLA Ops:
  1.3 0.8 %multiply_sine_fusion = (f32[64,64]{1,0:T(8,128)}, f32[64,64]{1,0:T(8,128)}) fusion(f32[64]{0:T(128)S(1)} %multiply_power_fusion, f32[64]{0:T(128)S(1)} %add_convert_fusion), kind=kLoop, calls=%fused_computation | loop fusion | flops 4096 | bytes 33280 | tf_op jit(solution)/shard_map/sin | solution.py:492
  2.1 49.5 %shard_map.140 = (bf16[64,2048]{1,0:T(8,128)(2,1)}, bf16[32,1024]{1,0:T(8,128)(2,1)}) custom-call(s32[1]{0:T(128)} %copy.17.length_ref, s32[1,16]{1,0:T(1,128)} %page_ref.1, bf16[64,2048]{1,0:T(8,128)(2,1)} %bitcast.18, bf16[64,512]{1,0:T(8,128)(2,1)} %bitcast.20, bf16[64,512]{1,0:T(8,128)(2,1)} %bitcast.21, bf16[512,512]{1,0:T(8,128)(2,1)} %bitcast.16, ...), custom_call_target="tpu_custom_call" | custom-call | tf_op jit(solution)/shard_map/pallas_call | solution.py:499
  51.7 1.7 %copy.18 = bf16[1,64,2048]{2,1,0:T(8,128)(2,1)} copy(bf16[1,64,2048]{2,1,0:T(8,128)(2,1)} %bitcast.19) | data formatting | bytes 524288
  53.3 1.5 %copy.19 = bf16[32,1024]{1,0:T(8,128)(2,1)} copy(bf16[32,1024]{1,0:T(8,128)(2,1)} %get-tuple-element.11) | data formatting | bytes 131072
  (2 shorter events, 0.0 us)
